TPU v7x, 32 devices: a whole 2x2x4 slice. The times are simulated.
32 devices in a mesh: req: 8 (over z, y), mlp: 4 (over x, core).
Axes of the slice: x: 2, y: 2, z: 4, core: 2. Of those that a mesh axis runs over, the one named last changes fastest.
Arguments:
- hidden: bfloat16 [4096, 3584], P('req', 'mlp'), may hold values from -6 to 6
- query_heads: bfloat16 [4096, 3584], P('req', 'mlp'), may hold values from -4 to 4
- key_heads: bfloat16 [4096, 3584], P('req', 'mlp'), may hold values from -4 to 4
- value_heads: bfloat16 [4096, 3584], P('req', 'mlp'), may hold values from -6 to 6
- segment_ids: int32 [4096], P('req'), may hold values from 0 to 31, never falling along the last dimension, each value on 1 to 1024 neighbouring positions
- page_table: int32 [8, 32], P('req'), may hold values from 0 to 31, each once within a row
- mamba_conv_input: bfloat16 [4096, 7168], P('req', 'mlp'), may hold values from -6 to 6
- mamba_output_gate: bfloat16 [4096, 7168], P('req', 'mlp'), may hold values from -6 to 6
- state_input_projection: bfloat16 [4096, 128], P('req'), may hold values from -6 to 6
- state_output_projection: bfloat16 [4096, 128], P('req'), may hold values from -6 to 6
- discrete_step_size: float32 [4096, 112], P('req', 'mlp'), may hold values from 0.24 to 100, as said below
- head_decay_rate: float32 [112], P('mlp'), may hold values from 0.00024414062 to 0.05, as said below
- skip_gain: float32 [112], P('mlp'), may hold values from 0.5 to 2
- mamba_gated_norm_gain: float32 [7168], P('mlp'), may hold values from 0.1 to 1.9
- attn_proj: bfloat16 [3584, 3584], P('mlp'), may hold values from -0.09375 to 0.09375
- mamba_output_projection: bfloat16 [7168, 3584], P('mlp'), may hold values from -0.0625 to 0.0625
- mlp_norm_gain: float32 [3584], replicated, may hold values from 0.1 to 1.9
- gate_proj: bfloat16 [3584, 7168], P('req', 'mlp'), may hold values from -0.09375 to 0.09375
- up_proj: bfloat16 [3584, 7168], P('req', 'mlp'), may hold values from -0.09375 to 0.09375
- down_proj: bfloat16 [7168, 3584], P('mlp', 'req'), may hold values from -0.0625 to 0.0625
- next_norm_gain: float32 [3584], P('mlp'), may hold values from 0.1 to 1.9
Outputs:
- new_hidden: bfloat16 [4096, 3584], P('req', 'mlp')
- next_normed: bfloat16 [4096, 3584], P('req', 'mlp')
- kv_cache: bfloat16 [2, 16, 256, 3584], P(None, 'mlp', 'req')
Inputs may be any that keep to these rules, and one draw needn't show every extreme that they name: `segment_ids`: prompt ids never fall along the stream; a prompt has 1 to 1024 tokens and one has exactly 1024. `page_table`: each request group's row names every page of its pool once. `discrete_step_size`: Positive. `head_decay_rate`: Positive.
All inputs are finite; a program needn't handle non-finite values.
Results may differ from a plain program's by a relative error of at most 0.006.
Values may be sent and summed in bfloat16 or wider, within the bound.
A program may use at most 192 MiB of HBM per device.

v0:
```python
import math

import jax
import jax.numpy as jnp
from jax import lax
from jax.sharding import PartitionSpec as P

HD = 224
MAMBA_HEAD_COUNT = 112
MAMBA_HEAD_SIZE = 64
STATE_SIZE = 64
STATE_GROUPS = 2
REACH = 2
PAGE = 16


EPSILON = 1e-05
exact_mode = lax.Precision.HIGHEST


def from_behind(value, axis, steps):
    count = lax.axis_size(axis)
    leading, last = (max(0, -steps), min(count, count - steps))
    return lax.ppermute(value, axis, [(source, source + steps) for source in range(leading, last)])


def entering(x, axis, combine, identity):
    devices, mine = (lax.axis_size(axis), lax.axis_index(axis))
    everything = jax.tree.map(lambda part: lax.all_gather(part, axis), x)
    start = jax.tree.map(
        lambda part, zero: jnp.broadcast_to(jnp.asarray(zero, part.dtype), part.shape), x, identity
    )

    def step(k, before):
        reached = k < mine
        new = combine(before, jax.tree.map(lambda part: part[k], everything))
        return jax.tree.map(lambda a, b: jnp.where(reached, a, b), new, before)

    return lax.fori_loop(0, devices, step, start)


def attend_rows(
    query_rows, segment_rows, pos_rows, all_keys, all_values, key_segs, key_pos, head_count
):
    row_total = query_rows.shape[0]
    key_total = all_keys.shape[0]
    query_split = query_rows.reshape(row_total, head_count, HD)
    key_split = all_keys.reshape(key_total, head_count, HD)
    value_split = all_values.reshape(key_total, head_count, HD)
    scores = jnp.einsum(
        "qhd,khd->hqk", query_split, key_split, preferred_element_type=jnp.float32
    ) * (1.0 / math.sqrt(HD))
    allowed = (segment_rows[:, None] == key_segs[None, :]) & (key_pos[None, :] <= pos_rows[:, None])
    scores = jnp.where(allowed[None, :, :], scores, -jnp.inf)
    top_score = jnp.max(scores, axis=2, keepdims=True)
    raised = jnp.exp(scores - top_score)
    weights = (raised / jnp.sum(raised, axis=2, keepdims=True)).astype(jnp.bfloat16)
    summed = jnp.einsum("hqk,khd->qhd", weights, value_split, preferred_element_type=jnp.float32)
    return summed.astype(jnp.bfloat16).reshape(row_total, head_count * HD)


def block_contributions(
    input_token_rows,
    input_proj_rows,
    output_proj_rows,
    step_size_rows,
    head_decay_rate,
    segment_rows,
    segment_prior_state,
    group_index,
    head_width,
):
    row_count = input_token_rows.shape[0]
    head_count = step_size_rows.shape[1]
    input_float = input_token_rows.astype(jnp.float32).reshape(row_count, head_count, head_width)
    b_float = input_proj_rows.astype(jnp.float32)
    c_float = output_proj_rows.astype(jnp.float32)
    running = jnp.cumsum(-step_size_rows * head_decay_rate[None, :], axis=0)
    positions = jnp.arange(row_count, dtype=jnp.int32)
    live = (segment_rows[:, None] == segment_rows[None, :]) & (
        positions[:, None] >= positions[None, :]
    )
    spread = running.T[:, :, None] - running.T[:, None, :]
    mixing = jnp.exp(jnp.where(live[None, :, :], spread, -1e30))
    inner = jnp.einsum("tgn,ugn->gtu", c_float, b_float, precision=exact_mode)
    driven = input_float * step_size_rows[:, :, None]
    local_output = jnp.einsum(
        "htu,uhp->thp", mixing * inner[group_index], driven, precision=exact_mode
    )
    b_per_head = b_float[:, group_index, :]
    output_proj_per_head = c_float[:, group_index, :]
    tail_rows = segment_rows == segment_rows[row_count - 1]
    tail_gain = jnp.where(
        tail_rows[:, None], jnp.exp(running[row_count - 1][None, :] - running), 0.0
    )
    state_local_part = jnp.einsum(
        "uh,uhp,uhn->hpn", tail_gain, driven, b_per_head, precision=exact_mode
    )
    decay_cumulative = jnp.where(
        segment_rows[row_count - 1] == segment_prior_state, jnp.exp(running[row_count - 1]), 0.0
    )
    entry_weighting = jnp.where(
        (segment_rows == segment_prior_state)[:, None], jnp.exp(running), 0.0
    )
    return (
        local_output,
        decay_cumulative,
        state_local_part,
        entry_weighting,
        input_float,
        output_proj_per_head,
    )


def finish(local_output, entry_weighting, input_float, output_proj_per_head, carry_in, skip_gain):
    carried = jnp.einsum("hpn,thn->thp", carry_in, output_proj_per_head, precision=exact_mode)
    result = (
        local_output
        + entry_weighting[:, :, None] * carried
        + skip_gain[None, :, None] * input_float
    )
    return result.reshape(result.shape[0], result.shape[1] * result.shape[2])


def merge_states(earlier, later):
    decay_early, state_early = earlier
    decay_late, state_late = later
    return (decay_early * decay_late, decay_late[:, None, None] * state_early + state_late)


def body(
    hidden,
    query_heads,
    key_heads,
    value_heads,
    segment_ids,
    page_table,
    mamba_conv_input,
    mamba_output_gate,
    state_input_projection,
    state_output_projection,
    discrete_step_size,
    head_decay_rate,
    skip_gain,
    mamba_gated_norm_gain,
    attn_proj,
    mamba_output_projection,
    mlp_norm_gain,
    gate_proj,
    up_proj,
    down_proj,
    next_norm_gain,
):
    row_count = query_heads.shape[0]
    head_count = query_heads.shape[1] // HD
    lane_count = hidden.shape[1]
    owner_index = lax.axis_index("req")
    column = lax.axis_index("mlp")
    first_row = owner_index * row_count
    lead_rows = REACH * row_count
    shifted_ids = segment_ids + 1
    key_parts = []
    value_parts = []
    segment_parts = []
    for distance in range(REACH, 0, -1):
        moved_ids = from_behind(shifted_ids, "req", distance)
        segment_parts.append(moved_ids - 1)
        moved_keys, moved_values = from_behind((key_heads, value_heads), "req", distance)
        key_parts.append(moved_keys)
        value_parts.append(moved_values)
    key_segs = jnp.concatenate(segment_parts + [segment_ids], axis=0)
    key_pos = first_row - lead_rows + jnp.arange(lead_rows + row_count, dtype=jnp.int32)
    segment_prior_state = segment_parts[-1][row_count - 1]
    all_keys = jnp.concatenate(key_parts + [key_heads], axis=0)
    all_values = jnp.concatenate(value_parts + [value_heads], axis=0)
    block_rows = min(row_count, 512)

    def one_block(block_index):
        first_local = block_index * block_rows
        pos_rows = first_row + first_local + jnp.arange(block_rows, dtype=jnp.int32)
        return attend_rows(
            query_heads, segment_ids, pos_rows, all_keys, all_values, key_segs, key_pos, head_count
        )

    attended = lax.map(one_block, jnp.arange(row_count // block_rows, dtype=jnp.int32)).reshape(
        row_count, head_count * HD
    )
    page_count = page_table.shape[1]
    key_pages = (
        key_heads.reshape(page_count, PAGE, head_count, HD)
        .transpose(2, 0, 1, 3)
        .reshape(head_count, page_count, PAGE * HD)
    )
    value_pages = (
        value_heads.reshape(page_count, PAGE, head_count, HD)
        .transpose(2, 0, 1, 3)
        .reshape(head_count, page_count, PAGE * HD)
    )
    stacked = jnp.stack([key_pages, value_pages])
    kv_cache = jnp.zeros_like(stacked).at[:, :, page_table[0]].set(stacked)
    mamba_heads = discrete_step_size.shape[1]
    group_values = MAMBA_HEAD_COUNT // STATE_GROUPS
    b_groups = state_input_projection.reshape(row_count, STATE_GROUPS, STATE_SIZE)
    c_groups = state_output_projection.reshape(row_count, STATE_GROUPS, STATE_SIZE)
    group_index = jnp.arange(mamba_heads, dtype=jnp.int32) % STATE_GROUPS
    (
        local_output,
        decay_cumulative,
        state_local_part,
        entry_weighting,
        input_float,
        output_proj_per_head,
    ) = block_contributions(
        mamba_conv_input,
        b_groups,
        c_groups,
        discrete_step_size,
        head_decay_rate,
        segment_ids,
        segment_prior_state,
        group_index,
        MAMBA_HEAD_SIZE,
    )
    unused_decay, carry_in = entering(
        (decay_cumulative, state_local_part),
        "req",
        merge_states,
        (jnp.ones_like(decay_cumulative), jnp.zeros_like(state_local_part)),
    )
    mamba_output = finish(
        local_output, entry_weighting, input_float, output_proj_per_head, carry_in, skip_gain
    )
    gated_output = mamba_output * jax.nn.silu(mamba_output_gate.astype(jnp.float32))
    grouped_values = gated_output.reshape(
        row_count, mamba_heads // STATE_GROUPS, STATE_GROUPS, MAMBA_HEAD_SIZE
    )
    group_squares = jnp.sum(grouped_values * grouped_values, axis=(1, 3))
    running_totals = lax.psum(group_squares, "mlp")
    inverse_group = lax.rsqrt(running_totals / (group_values * MAMBA_HEAD_SIZE) + EPSILON)
    mnormed = (
        (grouped_values * inverse_group[:, None, :, None]).reshape(
            row_count, mamba_heads * MAMBA_HEAD_SIZE
        )
        * mamba_gated_norm_gain[None, :]
    ).astype(jnp.bfloat16)
    projected = jnp.dot(attended, attn_proj, preferred_element_type=jnp.float32) + jnp.dot(
        mnormed, mamba_output_projection, preferred_element_type=jnp.float32
    )
    width_total = projected.shape[1]
    offset = column * lane_count
    own_part = lax.dynamic_slice_in_dim(projected, offset, lane_count, 1) + hidden.astype(
        jnp.float32
    )
    mixed_rows = lax.psum(lax.dynamic_update_slice_in_dim(projected, own_part, offset, 1), "mlp")
    mixed_share = lax.dynamic_slice_in_dim(mixed_rows, offset, lane_count, 1)
    inverse_root_mean = lax.rsqrt(jnp.mean(mixed_rows * mixed_rows, axis=1) + EPSILON)
    normed = (mixed_rows * inverse_root_mean[:, None] * mlp_norm_gain[None, :]).astype(jnp.bfloat16)
    gate_act = jnp.dot(
        normed,
        lax.all_gather(gate_proj, "req", axis=0, tiled=True),
        preferred_element_type=jnp.float32,
    )
    up_act = jnp.dot(
        normed,
        lax.all_gather(up_proj, "req", axis=0, tiled=True),
        preferred_element_type=jnp.float32,
    )
    latent_activation = (jax.nn.silu(gate_act) * up_act).astype(jnp.bfloat16)
    partial_value = jnp.dot(
        latent_activation,
        lax.all_gather(down_proj, "req", axis=1, tiled=True),
        preferred_element_type=jnp.float32,
    )
    mlp_share = lax.psum_scatter(partial_value, "mlp", scatter_dimension=1, tiled=True)
    new_hidden = (mixed_share + mlp_share).astype(jnp.bfloat16)
    widened = new_hidden.astype(jnp.float32)
    total_sq = lax.psum(jnp.sum(widened * widened, axis=1), "mlp")
    next_normed = (
        widened * lax.rsqrt(total_sq / width_total + EPSILON)[:, None] * next_norm_gain[None, :]
    ).astype(jnp.bfloat16)
    return (new_hidden, next_normed, kv_cache)


def solution(mesh):
    return jax.shard_map(
        body,
        mesh=mesh,
        in_specs=(
            P("req", "mlp"),
            P("req", "mlp"),
            P("req", "mlp"),
            P("req", "mlp"),
            P("req"),
            P("req", None),
            P("req", "mlp"),
            P("req", "mlp"),
            P("req", None),
            P("req", None),
            P("req", "mlp"),
            P("mlp"),
            P("mlp"),
            P("mlp"),
            P("mlp", None),
            P("mlp", None),
            P(),
            P("req", "mlp"),
            P("req", "mlp"),
            P("mlp", "req"),
            P("mlp"),
        ),
        out_specs=(P("req", "mlp"), P("req", "mlp"), P(None, "mlp", "req", None)),
        check_vma=False,
    )
```

profile of v0, /device:TPU:0, one launch (start us, length us, event | category | flops | bytes accessed | tf_op | source)
XLA Modules:
  0.0 1145.0 jit_solution(11778757619322424204)
XLA Ops:
  8.5 4.9 collective-permute-start.3
  27.4 4.9 fusion.22
  53.0 11.5 %gather_fusion = f32[28,512,512]{2,1,0:T(8,128)} fusion(f32[2,512,512]{2,1,0:T(8,128)S(1)} %fusion.54, s32[1024]{0:T(1024)} %copy-done.11), kind=kCustom, calls=%fused_computation | custom fusion | bytes 58720368 | tf_op jit(solution)/shard_map/gather | solution.py:88
  66.6 148.3 %all-gather.1 = f32[8,1,28]{2,1,0:T(1,128)S(1)} all-gather(f32[1,1,28]{2,1,0:T(1,128)} %bitcast.119), channel_id=1, replica_groups=mesh['req'=8,'mlp'=4] {'req'}, dimensions={0}, use_global_device_ids=true | all-gather | bytes 1008 | tf_op jit(solution)/shard_map/all_gather | solution.py:29
  233.0 11.0 fusion.52
  244.0 7.0 fusion.40
  251.0 8.8 fusion.53
  259.8 11.5 %while.18 = (s32[]{:T(128)}, f32[28,64,64]{2,1,0:T(8,128)S(1)}, s32[]{:T(128)}, f32[8,28]{1,0:T(8,128)S(1)}, f32[8,28,64,64]{3,2,1,0:T(8,128)}, /*index=5*/s32[]{:T(128)}, s32[]{:T(128)}) while((s32[]{:T(128)}, f32[28,64,64]{2,1,0:T(8,128)S(1)}, s32[]{:T(128)}, f32[8,28]{1,0:T(8,128)S(1)}, f32[8,28,64,64]{3,2,1,0:T(8,128)}, ...), condition=%wide.region_5.6_spmd.clone, body=%wide.region_4.5_spmd.clone.sunk | while | flops 458756 | bytes 1376697 | solution.py:39
  273.4 37.0 %fusion.21 = f32[512,28,64]{0,2,1:T(8,128)} fusion(f32[28,512,64]{1,2,0:T(8,128)S(1)} %fusion.34, f32[512,28,64]{0,2,1:T(8,128)S(1)} %bitcast.104, f32[28,512,512]{2,1,0:T(8,128)} %gather_fusion, f32[28,512]{1,0:T(8,128)S(1)} %bitcast.116, pred[512,512]{1,0:T(8,128)(4,1)S(1)} %fusion.41, f32[28]{0:T(128)S(1)} %copy-done.15, f32[512,28]{0,1:T(8,128)S(1)} %copy-done.9, ...), kind=kOutput, calls=%fused_computation.36 | convolution fusion | flops 5663752192 | bytes 40804464 | tf_op jit(solution)/shard_map/htu,uhp->thp/dot_general | solution.py:87
  310.4 5.3 copy.77
  315.7 4.8 fusion.50
  320.4 5.1 copy.78
  327.9 5.7 psum.21
  335.8 5.2 copy.79
  341.0 16.5 %convolution_add_fusion = f32[512,3584]{1,0:T(8,128)} fusion(f32[512,3584]{1,0:T(8,128)} %fusion.53, bf16[1792,3584]{1,0:T(8,128)(2,1)} %param.38, f32[512,1792]{1,0:T(8,128)} %copy.79, f32[1792]{0:T(1024)S(1)} %copy-done.14, f32[512,1792]{1,0:T(8,128)} %copy.77, bf16[512,1792]{1,0:T(8,128)(2,1)S(1)} %copy-done.4), kind=kOutput, calls=%fused_computation.27 | convolution fusion | flops 6586761216 | bytes 36707328 | tf_op jit(solution)/shard_map/dot_general | solution.py:246
  362.5 135.2 %all-reduce.2.cloned.1.call-done = f32[512,3584]{1,0:T(8,128)} async-done(((f32[512,3584]{1,0:T(8,128)}), f32[512,3584]{1,0:T(8,128)}) %all-reduce.2.cloned.1.call-update) | async-done | bytes 7340048 | tf_op jit(solution)/shard_map/psum | solution.py:254
  501.4 178.5 %all-gather.7.cloned.1.call-done = bf16[3584,1792]{1,0:T(8,128)(2,1)} async-done(((bf16[448,1792]{1,0:T(8,128)(2,1)}), bf16[3584,1792]{1,0:T(8,128)(2,1)}) %all-gather.7.cloned.1.call-update) | async-done | bytes 12845072 | tf_op jit(solution)/shard_map/all_gather | solution.py:260
  679.8 14.5 %fusion.51 = f32[512,1792]{1,0:T(8,128)} fusion(bf16[3584,1792]{1,0:T(8,128)(2,1)} %all-gather.7.cloned.1.call-done, f32[512,3584]{1,0:T(8,128)} %all-reduce.2.cloned.1.call-done, f32[3584]{0:T(1024)S(1)} %copy-done.13, f32[512]{0:T(512)S(1)} %add_rsqrt_fusion.2), kind=kOutput, calls=%fused_computation.93 | convolution fusion | flops 6582173696 | bytes 23871488 | tf_op jit(solution)/shard_map/dot_general | solution.py:258
  694.4 165.4 %all-gather.11.cloned.1.call-done = bf16[1792,3584]{0,1:T(8,128)(2,1)} async-done(((bf16[1792,448]{0,1:T(8,128)(2,1)}), bf16[1792,3584]{0,1:T(8,128)(2,1)}) %all-gather.11.cloned.1.call-update) | async-done | bytes 12845072 | tf_op jit(solution)/shard_map/all_gather | solution.py:271
  859.7 179.9 %all-gather.9.cloned.1.call-done = bf16[3584,1792]{1,0:T(8,128)(2,1)} async-done(((bf16[448,1792]{1,0:T(8,128)(2,1)}), bf16[3584,1792]{1,0:T(8,128)(2,1)}) %all-gather.9.cloned.1.call-update) | async-done | bytes 12845072 | tf_op jit(solution)/shard_map/all_gather | solution.py:265
  1039.6 25.2 %fusion.55 = f32[512,3584]{1,0:T(8,128)} fusion(bf16[1792,3584]{0,1:T(8,128)(2,1)} %all-gather.11.cloned.1.call-done, f32[512,1792]{1,0:T(8,128)} %fusion.51, bf16[3584,1792]{1,0:T(8,128)(2,1)} %all-gather.9.cloned.1.call-done, f32[512,3584]{1,0:T(8,128)} %all-reduce.2.cloned.1.call-done, f32[3584]{0:T(1024)S(1)} %copy-done.13, f32[512]{0:T(512)S(1)} %add_rsqrt_fusion.2), kind=kOutput, calls=%fused_computation.97 | convolution fusion | flops 13164347392 | bytes 44056576 | tf_op jit(solution)/shard_map/dot_general | solution.py:269
  1078.9 6.1 scatter_fusion
  1086.6 42.0 %reduce-scatter.2.cloned.1.call-done = f32[512,896]{1,0:T(8,128)} async-done(((f32[512,3584]{1,0:T(8,128)}), f32[512,896]{1,0:T(8,128)}) %reduce-scatter.2.cloned.1.call-update) | async-done | bytes 1835024 | tf_op jit(solution)/shard_map/reduce_scatter | solution.py:274
  1130.9 5.8 psum.23
  (132 shorter events, 100.2 us)
Async XLA Ops:
  7.2 252.7 %all-gather.13.cloned.1.call-start = ((), (), s32[]{:S(2)}) async-start(), calls=%async_computation.6 | async-start | bytes 8257536 | tf_op jit(solution)/shard_map/all_gather | solution.py:29
  8.5 14.4 %collective-permute-start.3 = (s32[512]{0:T(512)}, s32[512]{0:T(512)S(1)}, u32[]{:S(2)}, u32[]{:S(2)}) collective-permute-start(s32[512]{0:T(512)} %broadcast_add_fusion.3), channel_id=1, source_target_pairs={{0,4},{4,8},{8,12},{12,16},{16,20},{20,24},{24,28},{1,5},{5,9},{9,... | collective-permute-start | bytes 6152 | tf_op jit(solution)/shard_map/ppermute | solution.py:24
  15.8 7.1 copy-start.11
  22.2 5.2 copy-start.6
  22.9 9.5 copy-start.10
  27.4 22.7 %copy-start.7 = (bf16[512,128]{1,0:T(8,128)(2,1)S(1)}, bf16[512,128]{1,0:T(8,128)(2,1)}, u32[]{:S(2)}) copy-start(bf16[512,128]{1,0:T(8,128)(2,1)} %param.32) | copy-start | bytes 393220
  32.4 465.3 %all-reduce.2.cloned.1.call-start = ((), (), s32[]{:S(2)}) async-start(), calls=%async_computation.1 | async-start | bytes 14680064 | tf_op jit(solution)/shard_map/psum | solution.py:254
  32.4 33.5 %collective-permute-start.2 = (s32[512]{0:T(512)}, s32[512]{0:T(512)}, u32[]{:S(2)}, u32[]{:S(2)}) collective-permute-start(s32[512]{0:T(512)} %broadcast_add_fusion.3), channel_id=1, source_target_pairs={{0,8},{4,12},{8,16},{12,20},{16,24},{20,28},{1,9},{5,13},{9,17},{1... | collective-permute-start | bytes 6152 | tf_op jit(solution)/shard_map/ppermute | solution.py:24
  36.5 180.2 %collective-permute-start.4 = (bf16[512,896]{1,0:T(8,128)(2,1)}, bf16[512,896]{1,0:T(8,128)(2,1)}, u32[]{:S(2)}, u32[]{:S(2)}) collective-permute-start(bf16[512,896]{1,0:T(8,128)(2,1)} %param.25), channel_id=1, source_target_pairs={{0,8},{4,12},{8,16},{12,20},{16,24},{20,28},{1,9},{5,13},{9,17},{1... | collective-permute-start | bytes 2752520 | tf_op jit(solution)/shard_map/ppermute | solution.py:24
  40.4 176.4 %collective-permute-start.5 = (bf16[512,896]{1,0:T(8,128)(2,1)}, bf16[512,896]{1,0:T(8,128)(2,1)}, u32[]{:S(2)}, u32[]{:S(2)}) collective-permute-start(bf16[512,896]{1,0:T(8,128)(2,1)} %param.25), channel_id=1, source_target_pairs={{0,4},{4,8},{8,12},{12,16},{16,20},{20,24},{24,28},{1,5},{5,9},{9,... | collective-permute-start | bytes 2752520 | tf_op jit(solution)/shard_map/ppermute | solution.py:24
  44.8 180.1 %collective-permute-start = (bf16[512,896]{1,0:T(8,128)(2,1)}, bf16[512,896]{1,0:T(8,128)(2,1)}, u32[]{:S(2)}, u32[]{:S(2)}) collective-permute-start(bf16[512,896]{1,0:T(8,128)(2,1)} %param.26), channel_id=1, source_target_pairs={{0,8},{4,12},{8,16},{12,20},{16,24},{20,28},{1,9},{5,13},{9,17},{1... | collective-permute-start | bytes 2752520 | tf_op jit(solution)/shard_map/ppermute | solution.py:24
  47.0 177.8 %collective-permute-start.1 = (bf16[512,896]{1,0:T(8,128)(2,1)}, bf16[512,896]{1,0:T(8,128)(2,1)}, u32[]{:S(2)}, u32[]{:S(2)}) collective-permute-start(bf16[512,896]{1,0:T(8,128)(2,1)} %param.26), channel_id=1, source_target_pairs={{0,4},{4,8},{8,12},{12,16},{16,20},{20,24},{24,28},{1,5},{5,9},{9,... | collective-permute-start | bytes 2752520 | tf_op jit(solution)/shard_map/ppermute | solution.py:24
  259.8 11.5 %copy-start = (bf16[28,512,64]{1,2,0:T(8,128)(2,1)S(1)}, bf16[28,512,64]{1,2,0:T(8,128)(2,1)}, u32[]{:S(2)}) copy-start(bf16[28,512,64]{1,2,0:T(8,128)(2,1)} %gather_fusion.1) | copy-start | bytes 5505028
  310.4 5.3 copy-start.4
  335.8 5.2 copy-start.14
  341.0 16.6 %copy-start.5 = (bf16[512,896]{1,0:T(8,128)(2,1)S(1)}, bf16[512,896]{1,0:T(8,128)(2,1)}, u32[]{:S(2)}) copy-start(bf16[512,896]{1,0:T(8,128)(2,1)} %param.23) | copy-start | bytes 2752516
  360.5 319.3 %all-gather.7.cloned.1.call-start = ((), (), s32[]{:S(2)}) async-start(), calls=%async_computation.2 | async-start | bytes 14450688 | tf_op jit(solution)/shard_map/all_gather | solution.py:260
  361.3 498.4 %all-gather.11.cloned.1.call-start = ((), (), s32[]{:S(2)}) async-start(), calls=%async_computation.4 | async-start | bytes 14450688 | tf_op jit(solution)/shard_map/all_gather | solution.py:271
  361.8 677.8 %all-gather.9.cloned.1.call-start = ((), (), s32[]{:S(2)}) async-start(), calls=%async_computation.3 | async-start | bytes 14450688 | tf_op jit(solution)/shard_map/all_gather | solution.py:265
  362.4 317.4 %copy-start.13 = (f32[3584]{0:T(1024)S(1)}, f32[3584]{0:T(1024)}, u32[]{:S(2)}) copy-start(f32[3584]{0:T(1024)} %param.39) | copy-start | bytes 43012
  362.4 766.1 %reduce-scatter.2.cloned.1.call-start = ((), (), s32[]{:S(2)}) async-start(), calls=%async_computation.5 | async-start | bytes 9175040 | tf_op jit(solution)/shard_map/reduce_scatter | solution.py:274
  1071.2 4.8 copy-start.16
  1085.0 51.7 %copy-start.12 = (f32[896]{0:T(1024)S(1)}, f32[896]{0:T(1024)}, u32[]{:S(2)}) copy-start(f32[896]{0:T(1024)} %param.43) | copy-start | bytes 10756
  1130.9 7.0 copy-start.3
  (5 other events, 10.6 us)
Sparse Core Ops, SparseCore 0:
  32.5 140.8 all-gather.12
  360.7 137.0 all-reduce.1
  499.9 179.8 all-gather.6
  681.9 177.8 all-gather.10
  861.8 177.8 all-gather.8
  1064.9 63.6 reduce-scatter.1
where the time goes:
time: 1150 us; the launch traced here: 1140 us
  waiting for transfers between devices  703 us (61%)
  blocking collectives  160 us (14%)
  matrix products  127 us (11%)
  local copies, waits for them, and re-layouts  69.8 us (6%)
  other arithmetic  46.6 us (4%)
  starting transfers between devices  22.8 us (2%)
  between operations  16 us (1%)
    all_gather x1, waiting for transfers between devices, body(): lax.all_gather(up_proj, 'req', axis=0, tiled=True)  180 us
    all_gather x1, waiting for transfers between devices, body(): lax.all_gather(gate_proj, 'req', axis=0, tiled=True)  178 us
    all_gather x1, waiting for transfers between devices, body(): lax.all_gather(down_proj, 'req', axis=1, tiled=True)  165 us
    all_gather x1, blocking collectives, entering(): everything = jax.tree.map(lambda part: lax.all_gather(part, axis), x)  148 us
    psum x1, waiting for transfers between devices, body(): lax.psum(lax.dynamic_update_slice_in_dim(projected, own_part, offset, 1),...  135 us
    reduce_scatter x1, waiting for transfers between devices, body(): lax.psum_scatter(partial_value, 'mlp', scatter_dimension=1, tiled=True)  42 us
    dot_general x1, matrix products, block_contributions(): jnp.einsum('htu,uhp->thp', mixing * inner[group_index], driven, precision...  37 us
    dot_general x1, matrix products, body(): jnp.dot(latent_activation, lax.all_gather(down_proj, 'req', axis=1, tiled...  25.2 us
  transfers between devices with their start and end apart: 12, of which 5 were waited for; matrix products, arithmetic and copies ran while one was open for 10% of the time, Pallas kernels for 0%

commit v1 on v0

v1 whole, which is shorter than its diff:
```python
import math

import jax
import jax.numpy as jnp
from jax import lax
from jax.experimental import pallas as pl
from jax.experimental.pallas import tpu as pltpu
from jax.sharding import PartitionSpec as P

HD = 224
MAMBA_HEAD_COUNT = 112
MAMBA_HEAD_SIZE = 64
STATE_SIZE = 64
STATE_GROUPS = 2
REACH = 2
PAGE = 16
LANES = 128
CHUNK = 128
QUERY_BLOCK = 128

EPSILON = 1e-05
exact_mode = lax.Precision.HIGHEST


def from_behind(value, axis, steps):
    count = lax.axis_size(axis)
    return lax.ppermute(value, axis, [(source, source + steps) for source in range(count - steps)])


def weight_blocks(gate_proj, up_proj, down_proj):
    count = lax.axis_size("req")
    me = lax.axis_index("req")
    line = 4
    cross = count // line

    def exchange(value, flip):
        return lax.ppermute(value, "req", [(source, source ^ flip) for source in range(count)])

    own = (gate_proj, up_proj, down_proj.T)
    held = [(0, own)]
    for step in range(1, line):
        flip = step * cross
        held.append((flip, tuple(exchange(part, flip) for part in own)))
    blocks = list(held)
    for flip, block in held:
        for step in range(1, cross):
            blocks.append((flip ^ step, tuple(exchange(part, step) for part in block)))
    return [(jnp.bitwise_xor(me, flip), block) for flip, block in blocks]


def attention_kernel(q_ref, k2, k1, k0, v2, v1, v0, seg_q, seg_k, out_ref):
    rows = q_ref.shape[0]
    span = k0.shape[0]
    width = q_ref.shape[1]
    first = REACH * span + pl.program_id(0) * rows
    pos_q = first + lax.broadcasted_iota(jnp.int32, (rows, 1), 0)
    pos_k = lax.broadcasted_iota(jnp.int32, (1, (REACH + 1) * span), 1)
    allowed = (seg_q[...] == seg_k[...]) & (pos_k <= pos_q)
    bias = jnp.where(allowed, 0.0, -1e30)
    keys = (k2, k1, k0)
    values = (v2, v1, v0)
    tiles = [None] * (-(-width // LANES))
    for head in range(width // HD):
        low, high = head * HD, (head + 1) * HD
        start, stop = low // LANES * LANES, min(-(-high // LANES) * LANES, width)
        lane = start + lax.broadcasted_iota(jnp.int32, (1, stop - start), 1)
        inside = (lane >= low) & (lane < high)
        query = jnp.where(inside, q_ref[:, start:stop], jnp.zeros((), q_ref.dtype))
        scores = jnp.concatenate(
            [
                lax.dot_general(
                    query,
                    key[:, start:stop],
                    (((1,), (1,)), ((), ())),
                    preferred_element_type=jnp.float32,
                )
                for key in keys
            ],
            axis=1,
        )
        scores = scores * (1.0 / math.sqrt(HD)) + bias
        raised = jnp.exp(scores - jnp.max(scores, axis=1, keepdims=True))
        total = jnp.sum(raised, axis=1, keepdims=True)
        weights = raised.astype(jnp.bfloat16)
        summed = sum(
            jnp.dot(
                weights[:, part * span : (part + 1) * span],
                value[:, start:stop],
                preferred_element_type=jnp.float32,
            )
            for part, value in enumerate(values)
        )
        summed = jnp.where(inside, summed / total, 0.0)
        for tile in range(start // LANES, -(-stop // LANES)):
            piece = summed[:, tile * LANES - start : min((tile + 1) * LANES, stop) - start]
            tiles[tile] = piece if tiles[tile] is None else tiles[tile] + piece
    for tile, piece in enumerate(tiles):
        out_ref[:, tile * LANES : tile * LANES + piece.shape[1]] = piece.astype(out_ref.dtype)


def attention(query_heads, keys, values, segment_ids, key_segs):
    rows, width = query_heads.shape
    whole = pl.BlockSpec((rows, width), lambda i: (0, 0))
    block = pl.BlockSpec((QUERY_BLOCK, width), lambda i: (i, 0))
    reached = (REACH + 1) * rows
    return pl.pallas_call(
        attention_kernel,
        grid=(rows // QUERY_BLOCK,),
        in_specs=[block]
        + [whole] * 6
        + [
            pl.BlockSpec((QUERY_BLOCK, 1), lambda i: (i, 0)),
            pl.BlockSpec((1, reached), lambda i: (0, 0)),
        ],
        out_specs=block,
        out_shape=jax.ShapeDtypeStruct((rows, width), jnp.bfloat16),
        compiler_params=pltpu.CompilerParams(vmem_limit_bytes=48 * 2**20),
        cost_estimate=pl.CostEstimate(
            flops=4 * rows * reached * width * 8,
            bytes_accessed=16 * rows * width,
            transcendentals=rows * reached * 4,
        ),
        name="attention",
    )(query_heads, *keys, *values, segment_ids[:, None], key_segs[None, :])


def expand_matrix(heads):
    lane = jnp.arange(heads * MAMBA_HEAD_SIZE, dtype=jnp.int32)
    return (lane[None, :] // MAMBA_HEAD_SIZE == jnp.arange(heads)[:, None]).astype(jnp.float32)


def exact_dot(a, b):
    return jnp.dot(a, b, precision=exact_mode, preferred_element_type=jnp.float32)


def mamba_kernel(
    x_ref,
    gate_ref,
    b_ref,
    c_ref,
    run_ref,
    run_t,
    dt_t,
    entry_ref,
    tail_ref,
    decay_ref,
    skip_ref,
    expand_ref,
    seg_c,
    seg_r,
    carry_ref,
    gated_ref,
    squares_ref,
    state,
):
    rows, width = x_ref.shape

    @pl.when(pl.program_id(0) == 0)
    def _():
        state[...] = carry_ref[...]

    t_at = lax.broadcasted_iota(jnp.int32, (rows, rows), 0)
    u_at = lax.broadcasted_iota(jnp.int32, (rows, rows), 1)
    live = (seg_c[...] == seg_r[...]) & (u_at <= t_at)
    first_half = lax.broadcasted_iota(jnp.int32, (1, LANES), 1) < STATE_SIZE
    none = jnp.zeros((), jnp.bfloat16)
    b = b_ref[...]
    c = c_ref[...]
    inner = []
    for part in (first_half, ~first_half):
        product = lax.dot_general(
            jnp.where(part, c, none), b, (((1,), (1,)), ((), ())), preferred_element_type=jnp.float32
        )
        inner.append(jnp.where(live, product, 0.0))
    old = state[...]
    carried = jnp.dot(c, old.astype(jnp.bfloat16), preferred_element_type=jnp.float32)
    entry = exact_dot(entry_ref[...], expand_ref[...])
    tail = exact_dot(tail_ref[...], expand_ref[...])
    x = x_ref[...]
    weighted = (x.astype(jnp.float32) * tail).astype(jnp.bfloat16)
    added = lax.dot_general(
        b, weighted, (((0,), (0,)), ((), ())), preferred_element_type=jnp.float32
    )
    row_half = lax.broadcasted_iota(jnp.int32, (LANES, LANES), 0) < STATE_SIZE
    lane_half = lax.broadcasted_iota(jnp.int32, (LANES, LANES), 1) < STATE_SIZE
    same = row_half == lane_half
    squares = jnp.zeros((rows, LANES), jnp.float32)
    for pair in range(width // LANES):
        at = slice(pair * LANES, (pair + 1) * LANES)
        x_pair = x[:, at]
        y = entry[:, at] * carried[:, at] + skip_ref[:, at] * x_pair.astype(jnp.float32)
        for half in range(2):
            head = 2 * pair + half
            spread = run_ref[:, head : head + 1] - run_t[head : head + 1, :]
            mixing = jnp.exp(jnp.minimum(spread, 0.0)) * dt_t[head : head + 1, :] * inner[half]
            part = first_half if half == 0 else ~first_half
            y = y + jnp.dot(
                mixing.astype(jnp.bfloat16),
                jnp.where(part, x_pair, none),
                preferred_element_type=jnp.float32,
            )
        gate = gate_ref[:, at].astype(jnp.float32)
        gated = y * (gate / (1.0 + jnp.exp(-gate)))
        gated_ref[:, at] = gated
        squares = squares + gated * gated
        state[:, at] = decay_ref[0, :, at] * old[:, at] + jnp.where(same, added[:, at], 0.0)
    squares_ref[:, 0:1] = jnp.sum(jnp.where(first_half, squares, 0.0), axis=1, keepdims=True)
    squares_ref[:, 1:2] = jnp.sum(jnp.where(first_half, 0.0, squares), axis=1, keepdims=True)


def mamba(x, gate, b, c, dt, rate, skip_gain, segment_ids, prior_segment):
    rows, width = x.shape
    heads = dt.shape[1]
    expand = expand_matrix(heads)
    running = jnp.cumsum(-dt * rate[None, :], axis=0)
    last_segment = segment_ids[rows - 1]
    tail_rows = segment_ids == last_segment
    tail = jnp.where(tail_rows[:, None], jnp.exp(running[rows - 1][None, :] - running), 0.0) * dt
    lane = jnp.arange(width, dtype=jnp.int32)
    state_row = jnp.arange(STATE_GROUPS * STATE_SIZE, dtype=jnp.int32)
    own = (state_row[:, None] // STATE_SIZE) == (lane[None, :] // MAMBA_HEAD_SIZE % STATE_GROUPS)
    weighted = (x.astype(jnp.float32) * exact_dot(tail, expand)).astype(jnp.bfloat16)
    ends = lax.dot_general(b, weighted, (((0,), (0,)), ((), ())), preferred_element_type=jnp.float32)
    ends = jnp.where(own, ends, 0.0)
    ends = ends[:STATE_SIZE] + ends[STATE_SIZE:]
    decay = jnp.where(last_segment == prior_segment, jnp.exp(running[rows - 1]), 0.0)
    decay = exact_dot(decay[None, :], expand)
    nearer = from_behind(jnp.concatenate([ends, decay], axis=0), "req", 1)
    farther = from_behind(ends, "req", 2)
    carry = nearer[:STATE_SIZE] + nearer[STATE_SIZE:] * farther
    carry = jnp.where(own, jnp.concatenate([carry, carry], axis=0), 0.0)

    chunks = rows // CHUNK
    run_chunks = running.reshape(chunks, CHUNK, heads)
    seg_chunks = segment_ids.reshape(chunks, CHUNK)
    run_end = run_chunks[:, CHUNK - 1]
    seg_end = seg_chunks[:, CHUNK - 1]
    run_before = jnp.concatenate([jnp.zeros_like(run_end[:1]), run_end[:-1]], axis=0)
    seg_before = jnp.concatenate([prior_segment[None], seg_end[:-1]], axis=0)
    entry = jnp.where(
        (seg_chunks == seg_before[:, None])[:, :, None],
        jnp.exp(run_chunks - run_before[:, None]),
        0.0,
    ).reshape(rows, heads)
    chunk_tail = jnp.where(
        (seg_chunks == seg_end[:, None])[:, :, None], jnp.exp(run_end[:, None] - run_chunks), 0.0
    ).reshape(rows, heads) * dt
    chunk_decay = jnp.where((seg_end == seg_before)[:, None], jnp.exp(run_end - run_before), 0.0)
    chunk_decay = exact_dot(chunk_decay, expand)[:, None, :]
    skip = exact_dot(skip_gain[None, :], expand)

    def by_row(columns):
        return pl.BlockSpec((CHUNK, columns), lambda i: (i, 0))

    def by_lane(count):
        return pl.BlockSpec((count, CHUNK), lambda i: (0, i))

    def whole(shape):
        return pl.BlockSpec(shape, lambda i: (0, 0))

    return pl.pallas_call(
        mamba_kernel,
        grid=(chunks,),
        in_specs=[
            by_row(width),
            by_row(width),
            by_row(LANES),
            by_row(LANES),
            by_row(heads),
            by_lane(heads),
            by_lane(heads),
            by_row(heads),
            by_row(heads),
            pl.BlockSpec((1, 1, width), lambda i: (i, 0, 0)),
            whole((1, width)),
            whole((heads, width)),
            by_row(1),
            by_lane(1),
            whole((LANES, width)),
        ],
        out_specs=[by_row(width), by_row(STATE_GROUPS)],
        out_shape=[
            jax.ShapeDtypeStruct((rows, width), jnp.float32),
            jax.ShapeDtypeStruct((rows, STATE_GROUPS), jnp.float32),
        ],
        scratch_shapes=[pltpu.VMEM((LANES, width), jnp.float32)],
        compiler_params=pltpu.CompilerParams(vmem_limit_bytes=48 * 2**20),
        cost_estimate=pl.CostEstimate(
            flops=rows * width * 4000, bytes_accessed=rows * width * 10, transcendentals=rows * width * 2
        ),
        name="mamba",
    )(
        x,
        gate,
        b,
        c,
        running,
        running.T,
        dt.T,
        entry,
        chunk_tail,
        chunk_decay,
        skip,
        expand,
        segment_ids[:, None],
        segment_ids[None, :],
        carry,
    )


def body(
    hidden,
    query_heads,
    key_heads,
    value_heads,
    segment_ids,
    page_table,
    mamba_conv_input,
    mamba_output_gate,
    state_input_projection,
    state_output_projection,
    discrete_step_size,
    head_decay_rate,
    skip_gain,
    mamba_gated_norm_gain,
    attn_proj,
    mamba_output_projection,
    mlp_norm_gain,
    gate_proj,
    up_proj,
    down_proj,
    next_norm_gain,
):
    row_count, lane_count = hidden.shape
    head_count = query_heads.shape[1] // HD
    width_total = attn_proj.shape[1]
    mamba_width = mamba_conv_input.shape[1]
    column = lax.axis_index("mlp")

    segment_parts = []
    key_parts = []
    value_parts = []
    for distance in range(REACH, 0, -1):
        segment_parts.append(from_behind(segment_ids + 1, "req", distance) - 1)
        key_parts.append(from_behind(key_heads, "req", distance))
        value_parts.append(from_behind(value_heads, "req", distance))
    key_segs = jnp.concatenate(segment_parts + [segment_ids], axis=0)
    prior_segment = segment_parts[-1][row_count - 1]

    blocks = weight_blocks(gate_proj, up_proj, down_proj)

    gated, squares = mamba(
        mamba_conv_input,
        mamba_output_gate,
        state_input_projection,
        state_output_projection,
        discrete_step_size,
        head_decay_rate,
        skip_gain,
        segment_ids,
        prior_segment,
    )
    totals = lax.psum(squares, "mlp")
    attended = attention(
        query_heads, key_parts + [key_heads], value_parts + [value_heads], segment_ids, key_segs
    )

    page_count = page_table.shape[1]
    pages = jnp.arange(page_count, dtype=jnp.int32)
    source_page = jnp.sum(
        jnp.where(page_table[0][None, :] == pages[:, None], pages[None, :], 0), axis=1
    )

    def cache_of(heads):
        ordered = heads.reshape(page_count, PAGE, head_count * HD)[source_page]
        return (
            ordered.reshape(page_count, PAGE, head_count, HD)
            .transpose(2, 0, 1, 3)
            .reshape(head_count, page_count, PAGE * HD)
        )

    kv_cache = jnp.stack([cache_of(key_heads), cache_of(value_heads)])

    inverse_group = lax.rsqrt(totals / (MAMBA_HEAD_COUNT // STATE_GROUPS * MAMBA_HEAD_SIZE) + EPSILON)
    first_group = jnp.arange(mamba_width, dtype=jnp.int32) // MAMBA_HEAD_SIZE % STATE_GROUPS == 0
    scale = jnp.where(first_group[None, :], inverse_group[:, 0:1], inverse_group[:, 1:2])
    mnormed = (gated * scale * mamba_gated_norm_gain[None, :]).astype(jnp.bfloat16)
    projected = jnp.dot(attended, attn_proj, preferred_element_type=jnp.float32) + jnp.dot(
        mnormed, mamba_output_projection, preferred_element_type=jnp.float32
    )
    mixed = lax.psum_scatter(
        projected, "mlp", scatter_dimension=1, tiled=True
    ) + hidden.astype(jnp.float32)
    mixed_squares = lax.psum(jnp.sum(mixed * mixed, axis=1), "mlp")
    own_gain = lax.dynamic_slice_in_dim(mlp_norm_gain, column * lane_count, lane_count)
    scaled = (mixed * own_gain[None, :]).astype(jnp.bfloat16)
    rows_all = lax.all_gather(scaled, "mlp", axis=1, tiled=True)
    inverse = lax.rsqrt(mixed_squares / width_total + EPSILON)[:, None]
    depth = gate_proj.shape[0]
    gate_sum = None
    up_sum = None
    for owner, block in blocks:
        part = lax.dynamic_slice_in_dim(rows_all, owner * depth, depth, 1)
        gate_part = jnp.dot(part, block[0], preferred_element_type=jnp.float32)
        up_part = jnp.dot(part, block[1], preferred_element_type=jnp.float32)
        gate_sum = gate_part if gate_sum is None else gate_sum + gate_part
        up_sum = up_part if up_sum is None else up_sum + up_part
    latent = (jax.nn.silu(gate_sum * inverse) * (up_sum * inverse)).astype(jnp.bfloat16)
    down_all = jnp.zeros((width_total, latent.shape[1]), jnp.bfloat16)
    for owner, block in blocks:
        down_all = lax.dynamic_update_slice_in_dim(down_all, block[2], owner * depth, 0)
    partial_value = lax.dot_general(
        latent, down_all, (((1,), (1,)), ((), ())), preferred_element_type=jnp.float32
    )
    mlp_share = lax.psum_scatter(
        partial_value.astype(jnp.bfloat16), "mlp", scatter_dimension=1, tiled=True
    )
    new_hidden = (mixed + mlp_share.astype(jnp.float32)).astype(jnp.bfloat16)
    widened = new_hidden.astype(jnp.float32)
    total_sq = lax.psum(jnp.sum(widened * widened, axis=1), "mlp")
    next_normed = (
        widened * lax.rsqrt(total_sq / width_total + EPSILON)[:, None] * next_norm_gain[None, :]
    ).astype(jnp.bfloat16)
    return (new_hidden, next_normed, kv_cache)


def solution(mesh):
    return jax.shard_map(
        body,
        mesh=mesh,
        in_specs=(
            P("req", "mlp"),
            P("req", "mlp"),
            P("req", "mlp"),
            P("req", "mlp"),
            P("req"),
            P("req", None),
            P("req", "mlp"),
            P("req", "mlp"),
            P("req", None),
            P("req", None),
            P("req", "mlp"),
            P("mlp"),
            P("mlp"),
            P("mlp"),
            P("mlp", None),
            P("mlp", None),
            P(),
            P("req", "mlp"),
            P("req", "mlp"),
            P("mlp", "req"),
            P("mlp"),
        ),
        out_specs=(P("req", "mlp"), P("req", "mlp"), P(None, "mlp", "req", None)),
        check_vma=False,
    )
```

time: 1150 us -> 919 us (0.80)
  waiting for transfers between devices: 703 us -> 512 us
  starting transfers between devices: 22.8 us -> 158 us
  blocking collectives: 160 us -> 25 us
  other arithmetic: 46.6 us -> 17.1 us
  Pallas kernels: 0 us -> 27.2 us
  matrix products: 127 us -> 105 us
  local copies, waits for them, and re-layouts: 69.8 us -> 52.4 us
    all_gather x4 -> x1, waiting for transfers between devices: 524 us -> 0.02 us  [body(): rows_all = lax.all_gather(scaled, 'mlp', axis=1, tiled=True)]
    ppermute x6 -> x29, waiting for transfers between devices: 0.02 us -> 421 us  [the longest x21 412 us: exchange(): lax.ppermute(value, 'req', [(source, source ^ flip) for source in range(c...]
    all_gather x1 -> x0, blocking collectives: 148 us -> none  [entering(): everything = jax.tree.map(lambda part: lax.all_gather(part, axis), x)]
    psum x1 -> x0, waiting for transfers between devices: 135 us -> none  [body(): lax.psum(lax.dynamic_update_slice_in_dim(projected, own_part, offset, 1),...]
    ppermute x6 -> x29, starting transfers between devices: 22.5 us -> 157 us  [the longest x21 102 us: exchange(): lax.ppermute(value, 'req', [(source, source ^ flip) for source in range(c...]
    pallas_call x0 -> x2, Pallas kernels: none -> 27.2 us  [the longest x1 15 us: attention(): pl.pallas_call(attention_kernel, grid=(rows // QUERY_BLOCK,), in_specs=[b...]
    unnamed x6 -> x4, waiting for transfers between devices: 1.79 us -> 25.6 us
    reduce_scatter x1, waiting for transfers between devices: 42 us -> 65.5 us  [body(): lax.psum_scatter(projected, 'mlp', scatter_dimension=1, tiled=True)]
  transfers between devices with their start and end apart: 12 -> 32, of which waited for: 5 -> 13; matrix products, arithmetic and copies ran while one was open for 10% -> 13% of each run, Pallas kernels for 0% -> 1%
where the time goes in v1:
time: 919 us; the launch traced here: 912 us
  waiting for transfers between devices  512 us (56%)
  starting transfers between devices  158 us (17%)
  matrix products  105 us (11%)
  local copies, waits for them, and re-layouts  52.4 us (6%)
  Pallas kernels  27.2 us (3%)
  blocking collectives  25 us (3%)
  other arithmetic  17.1 us (2%)
  between operations  16.1 us (2%)
    ppermute x21, waiting for transfers between devices, exchange(): lax.ppermute(value, 'req', [(source, source ^ flip) for source in range(c...  412 us
    ppermute x21, starting transfers between devices, exchange(): lax.ppermute(value, 'req', [(source, source ^ flip) for source in range(c...  102 us
    reduce_scatter x1, waiting for transfers between devices, body(): lax.psum_scatter(projected, 'mlp', scatter_dimension=1, tiled=True)  65.5 us
    ppermute x8, starting transfers between devices, from_behind(): lax.ppermute(value, axis, [(source, source + steps) for source in range(c...  55.9 us
    dot_general x8, matrix products, body(): up_part = jnp.dot(part, block[1], preferred_element_type=jnp.float32)  31.5 us
    dot_general x1, matrix products, body(): lax.dot_general(latent, down_all, (((1,), (1,)), ((), ())), preferred_ele...  26.9 us
    unnamed x4, waiting for transfers between devices  25.6 us
    dot_general x7, matrix products, body(): gate_part = jnp.dot(part, block[0], preferred_element_type=jnp.float32)  22.7 us
  transfers between devices with their start and end apart: 32, of which 13 were waited for; matrix products, arithmetic and copies ran while one was open for 13% of the time, Pallas kernels for 1%

profile of v1, /device:TPU:0, one launch (start us, length us, event | category | flops | bytes accessed | tf_op | source)
XLA Modules:
  0.0 912.2 jit_solution(14082721148837965776)
XLA Ops:
  7.2 6.0 collective-permute-start
  42.8 21.1 %collective-permute-start.7 = (f32[64,1792]{1,0:T(8,128)S(1)}, f32[64,1792]{1,0:T(8,128)S(1)}, u32[]{:S(2)}, u32[]{:S(2)}) collective-permute-start(f32[64,1792]{1,0:T(8,128)S(1)} %slice_add_fusion.1), channel_id=1, source_target_pairs={{0,8},{4,12},{8,16},{12,20},{16,24},{20,28},{1,9},{5,13},{9,17},{1... | collective-permute-start | bytes 1376264 | tf_op jit(solution)/shard_map/ppermute | solution.py:27
  75.4 13.0 %collective-permute-start.3 = (bf16[512,896]{1,0:T(8,128)(2,1)}, bf16[512,896]{1,0:T(8,128)(2,1)}, u32[]{:S(2)}, u32[]{:S(2)}) collective-permute-start(bf16[512,896]{1,0:T(8,128)(2,1)} %v0.1), channel_id=1, source_target_pairs={{0,4},{4,8},{8,12},{12,16},{16,20},{20,24},{24,28},{1,5},{5,9},{9,... | collective-permute-start | bytes 2752520 | tf_op jit(solution)/shard_map/ppermute | solution.py:27
  88.7 12.1 %mamba.1 = (f32[512,1792]{1,0:T(8,128)}, f32[512,2]{1,0:T(8,128)S(1)}) custom-call(bf16[512,1792]{1,0:T(8,128)(2,1)S(1)} %copy-done.2, bf16[512,1792]{1,0:T(8,128)(2,1)} %gate_ref.1, bf16[512,128]{1,0:T(8,128)(2,1)S(1)} %copy-done.5, bf16[512,128]{1,0:T(8,128)(2,1)S(1)} %copy-done.8, f32[512,28]{1,0:T(8,128)S(1)} %bitcast.103, f32[28,512]{1,0:T(8,128)S(1)} %copy.71.run_t, ...), custom_call_target="tpu_custom_call" | custom-call | flops 3670016000 | bytes 9175040 | tf_op jit(solution)/shard_map/mamba/pallas_call | solution.py:261
  100.8 13.1 %psum.21 = f32[512,2]{1,0:T(8,128)S(1)} all-reduce(f32[512,2]{1,0:T(8,128)S(1)} %get-tuple-element.6), channel_id=1, replica_groups=mesh['req'=8,'mlp'=4] {'mlp'}, use_global_device_ids=true, to_apply=%region_2.3 | all-reduce | flops 1024 | bytes 8192 | tf_op jit(solution)/shard_map/psum | solution.py:363
  114.3 13.0 %fusion.4 = f32[512,3584]{1,0:T(8,128)} fusion(bf16[1792,3584]{1,0:T(8,128)(2,1)} %param.36, f32[512,1792]{1,0:T(8,128)} %get-tuple-element.5, f32[1792]{0:T(1024)S(1)} %copy-done.15, f32[512]{0:T(512)S(1)} %get-tuple-element.8, f32[512]{0:T(512)S(1)} %get-tuple-element.7, pred[1792]{0:T(1024)(128)(4,1)S(1)} %broadcast_compare_fusion), kind=kOutput, calls=%fused_computation.14 | convolution fusion | flops 6580338688 | bytes 23868160 | tf_op jit(solution)/shard_map/dot_general | solution.py:388
  127.3 15.0 %attention.1 = bf16[512,896]{1,0:T(8,128)(2,1)S(1)} custom-call(bf16[512,896]{1,0:T(8,128)(2,1)S(1)} %copy-done.7, bf16[512,896]{1,0:T(8,128)(2,1)} %collective-permute-done.k2, bf16[512,896]{1,0:T(8,128)(2,1)} %collective-permute-done.1.k1, bf16[512,896]{1,0:T(8,128)(2,1)S(1)} %copy-done.3, bf16[512,896]{1,0:T(8,128)(2,1)} %collective-permute-done.2.v2, ...), custom_call_target="tpu_custom_call" | custom-call | flops 22548578304 | bytes 7340032 | tf_op jit(solution)/shard_map/attention/pallas_call | solution.py:106
  142.4 8.1 convolution_add_fusion
  151.5 65.5 %reduce-scatter.5.cloned.1.call-done = f32[512,896]{1,0:T(8,128)} async-done(((f32[512,3584]{1,0:T(8,128)}), f32[512,896]{1,0:T(8,128)}) %reduce-scatter.5.cloned.1.call-update) | async-done | bytes 1835024 | tf_op jit(solution)/shard_map/reduce_scatter | solution.py:391
  229.2 61.3 %collective-permute-done.22 = bf16[448,1792]{1,0:T(8,128)(2,1)} collective-permute-done((bf16[448,1792]{1,0:T(8,128)(2,1)S(1)}, bf16[448,1792]{1,0:T(8,128)(2,1)}, u32[]{:S(2)}, u32[]{:S(2)}) %collective-permute-start.22) | collective-permute-done | bytes 1605664 | tf_op jit(solution)/shard_map/ppermute | solution.py:37
  292.0 71.7 %collective-permute-done.23 = bf16[448,1792]{1,0:T(8,128)(2,1)} collective-permute-done((bf16[448,1792]{1,0:T(8,128)(2,1)S(1)}, bf16[448,1792]{1,0:T(8,128)(2,1)}, u32[]{:S(2)}, u32[]{:S(2)}) %collective-permute-start.23) | collective-permute-done | bytes 1605664 | tf_op jit(solution)/shard_map/ppermute | solution.py:37
  380.5 28.7 %collective-permute-start.16 = (bf16[448,1792]{1,0:T(8,128)(2,1)}, bf16[448,1792]{1,0:T(8,128)(2,1)}, u32[]{:S(2)}, u32[]{:S(2)}) collective-permute-start(bf16[448,1792]{1,0:T(8,128)(2,1)} %param.39), channel_id=1, source_target_pairs={{0,16},{4,20},{8,24},{12,28},{16,0},{20,4},{24,8},{28,12},{1,17},{... | collective-permute-start | bytes 4816904 | tf_op jit(solution)/shard_map/ppermute | solution.py:37
  419.0 49.4 %collective-permute-start.9 = (bf16[448,1792]{1,0:T(8,128)(2,1)}, bf16[448,1792]{1,0:T(8,128)(2,1)}, u32[]{:S(2)}, u32[]{:S(2)}) collective-permute-start(bf16[448,1792]{1,0:T(8,128)(2,1)} %param.38), channel_id=1, source_target_pairs={{0,16},{4,20},{8,24},{12,28},{16,0},{20,4},{24,8},{28,12},{1,17},{... | collective-permute-start | bytes 4816904 | tf_op jit(solution)/shard_map/ppermute | solution.py:37
  471.2 6.3 psum.22
  486.7 83.4 %collective-permute-done.16 = bf16[448,1792]{1,0:T(8,128)(2,1)} collective-permute-done((bf16[448,1792]{1,0:T(8,128)(2,1)}, bf16[448,1792]{1,0:T(8,128)(2,1)}, u32[]{:S(2)}, u32[]{:S(2)}) %collective-permute-start.16) | collective-permute-done | bytes 1605664 | tf_op jit(solution)/shard_map/ppermute | solution.py:37
  590.1 47.6 %collective-permute-done.9 = bf16[448,1792]{1,0:T(8,128)(2,1)} collective-permute-done((bf16[448,1792]{1,0:T(8,128)(2,1)}, bf16[448,1792]{1,0:T(8,128)(2,1)}, u32[]{:S(2)}, u32[]{:S(2)}) %collective-permute-start.9) | collective-permute-done | bytes 1605664 | tf_op jit(solution)/shard_map/ppermute | solution.py:37
  655.0 26.6 %collective-permute-done.18 = bf16[448,1792]{1,0:T(8,128)(2,1)S(1)} collective-permute-done((bf16[448,1792]{1,0:T(8,128)(2,1)}, bf16[448,1792]{1,0:T(8,128)(2,1)S(1)}, u32[]{:S(2)}, u32[]{:S(2)}) %collective-permute-start.18) | collective-permute-done | bytes 1605664 | tf_op jit(solution)/shard_map/ppermute | solution.py:37
  684.7 31.4 %collective-permute-done.14 = bf16[448,1792]{1,0:T(8,128)(2,1)S(1)} collective-permute-done((bf16[448,1792]{1,0:T(8,128)(2,1)S(1)}, bf16[448,1792]{1,0:T(8,128)(2,1)S(1)}, u32[]{:S(2)}, u32[]{:S(2)}) %collective-permute-start.14) | collective-permute-done | bytes 1605664 | tf_op jit(solution)/shard_map/ppermute | solution.py:37
  719.1 31.4 %collective-permute-done.13 = bf16[448,1792]{1,0:T(8,128)(2,1)S(1)} collective-permute-done((bf16[448,1792]{1,0:T(8,128)(2,1)}, bf16[448,1792]{1,0:T(8,128)(2,1)S(1)}, u32[]{:S(2)}, u32[]{:S(2)}) %collective-permute-start.13) | collective-permute-done | bytes 1605664 | tf_op jit(solution)/shard_map/ppermute | solution.py:37
  753.5 31.4 %collective-permute-done.12 = bf16[448,1792]{1,0:T(8,128)(2,1)S(1)} collective-permute-done((bf16[448,1792]{1,0:T(8,128)(2,1)S(1)}, bf16[448,1792]{1,0:T(8,128)(2,1)S(1)}, u32[]{:S(2)}, u32[]{:S(2)}) %collective-permute-start.12) | collective-permute-done | bytes 1605664 | tf_op jit(solution)/shard_map/ppermute | solution.py:37
  788.2 27.3 %collective-permute-done.11 = bf16[448,1792]{1,0:T(8,128)(2,1)S(1)} collective-permute-done((bf16[448,1792]{1,0:T(8,128)(2,1)}, bf16[448,1792]{1,0:T(8,128)(2,1)S(1)}, u32[]{:S(2)}, u32[]{:S(2)}) %collective-permute-start.11) | collective-permute-done | bytes 1605664 | tf_op jit(solution)/shard_map/ppermute | solution.py:37
  818.5 26.9 %convolution_convert_fusion = bf16[512,3584]{1,0:T(8,128)(2,1)} fusion(bf16[3584,1792]{1,0:T(8,128)(2,1)} %constant_dynamic-update-slice_fusion, f32[512,1792]{1,0:T(8,128)} %fusion.11, f32[512,1792]{1,0:T(8,128)} %fusion.15, f32[512,1792]{1,0:T(8,128)} %fusion.19, f32[512,1792]{1,0:T(8,128)} %fusion.23, f32[512,1792]{1,0:T(8,128)} %fusion.27, ...), kind=kOutput, calls=%fused_computation.3 | convolution fusion | flops 7420772352 | bytes 73697280 | tf_op jit(solution)/shard_map/dot_general | solution.py:412
  845.4 5.9 copy.77
  866.6 25.5 %reduce-scatter.7.cloned.1.call-done = bf16[896,512]{1,0:T(8,128)(2,1)} async-done(((bf16[3584,512]{1,0:T(8,128)(2,1)}), bf16[896,512]{1,0:T(8,128)(2,1)}) %reduce-scatter.7.cloned.1.call-update) | async-done | bytes 917520
  (184 shorter events, 174.1 us)
Async XLA Ops:
  7.2 209.8 %reduce-scatter.5.cloned.1.call-start = ((), (), s32[]{:S(2)}) async-start(), calls=%async_computation.2 | async-start | bytes 9175040 | tf_op jit(solution)/shard_map/reduce_scatter | solution.py:391
  7.2 120.1 %collective-permute-start = (bf16[512,896]{1,0:T(8,128)(2,1)}, bf16[512,896]{1,0:T(8,128)(2,1)}, u32[]{:S(2)}, u32[]{:S(2)}) collective-permute-start(bf16[512,896]{1,0:T(8,128)(2,1)} %k0.1), channel_id=1, source_target_pairs={{0,8},{4,12},{8,16},{12,20},{16,24},{20,28},{1,9},{5,13},{9,17},{1... | collective-permute-start | bytes 2752520 | tf_op jit(solution)/shard_map/ppermute | solution.py:27
  13.2 114.1 %collective-permute-start.1 = (bf16[512,896]{1,0:T(8,128)(2,1)}, bf16[512,896]{1,0:T(8,128)(2,1)}, u32[]{:S(2)}, u32[]{:S(2)}) collective-permute-start(bf16[512,896]{1,0:T(8,128)(2,1)} %k0.1), channel_id=1, source_target_pairs={{0,4},{4,8},{8,12},{12,16},{16,20},{20,24},{24,28},{1,5},{5,9},{9,... | collective-permute-start | bytes 2752520 | tf_op jit(solution)/shard_map/ppermute | solution.py:27
  150.6 326.9 %all-gather.2.cloned.1.call-start = ((), (), s32[]{:S(2)}) async-start(), calls=%async_computation.3 | async-start | bytes 4587520 | tf_op jit(solution)/shard_map/all_gather | solution.py:397
  219.8 672.3 %reduce-scatter.7.cloned.1.call-start = ((), (), s32[]{:S(2)}) async-start(), calls=%async_computation.4 | async-start | bytes 4587520
  221.5 142.3 %collective-permute-start.23 = (bf16[448,1792]{1,0:T(8,128)(2,1)S(1)}, bf16[448,1792]{1,0:T(8,128)(2,1)}, u32[]{:S(2)}, u32[]{:S(2)}) collective-permute-start(bf16[448,1792]{1,0:T(8,128)(2,1)S(1)} %bitcast.117), channel_id=1, source_target_pairs={{0,16},{4,20},{8,24},{12,28},{16,0},{20,4},{24,8},{28,12},{1,17},{... | collective-permute-start | bytes 4816904 | tf_op jit(solution)/shard_map/ppermute | solution.py:37
  223.9 148.0 %collective-permute-start.24 = (bf16[448,1792]{1,0:T(8,128)(2,1)S(1)}, bf16[448,1792]{1,0:T(8,128)(2,1)}, u32[]{:S(2)}, u32[]{:S(2)}) collective-permute-start(bf16[448,1792]{1,0:T(8,128)(2,1)S(1)} %bitcast.118), channel_id=1, source_target_pairs={{0,24},{4,28},{8,16},{12,20},{16,8},{20,12},{24,0},{28,4},{1,25},{... | collective-permute-start | bytes 4816904 | tf_op jit(solution)/shard_map/ppermute | solution.py:37
  224.3 156.1 %collective-permute-start.25 = (bf16[448,1792]{1,0:T(8,128)(2,1)S(1)}, bf16[448,1792]{1,0:T(8,128)(2,1)}, u32[]{:S(2)}, u32[]{:S(2)}) collective-permute-start(bf16[448,1792]{1,0:T(8,128)(2,1)S(1)} %bitcast.119), channel_id=1, source_target_pairs={{0,4},{4,0},{8,12},{12,8},{16,20},{20,16},{24,28},{28,24},{1,5},{5... | collective-permute-start | bytes 4816904 | tf_op jit(solution)/shard_map/ppermute | solution.py:37
  225.8 193.1 %collective-permute-start.17 = (bf16[448,1792]{1,0:T(8,128)(2,1)}, bf16[448,1792]{1,0:T(8,128)(2,1)}, u32[]{:S(2)}, u32[]{:S(2)}) collective-permute-start(bf16[448,1792]{1,0:T(8,128)(2,1)} %param.39), channel_id=1, source_target_pairs={{0,24},{4,28},{8,16},{12,20},{16,8},{20,12},{24,0},{28,4},{1,25},{... | collective-permute-start | bytes 4816904 | tf_op jit(solution)/shard_map/ppermute | solution.py:37
  290.5 121.3 %collective-permute-start.26 = (bf16[448,1792]{1,0:T(8,128)(2,1)}, bf16[448,1792]{1,0:T(8,128)(2,1)}, u32[]{:S(2)}, u32[]{:S(2)}) collective-permute-start(bf16[448,1792]{1,0:T(8,128)(2,1)} %collective-permute-done.22), channel_id=1, source_target_pairs={{0,4},{4,0},{8,12},{12,8},{16,20},{20,16},{24,28},{28,24},{1,5},{5... | collective-permute-start | bytes 4816904 | tf_op jit(solution)/shard_map/ppermute | solution.py:37
  371.9 96.5 %collective-permute-start.28 = (bf16[448,1792]{1,0:T(8,128)(2,1)}, bf16[448,1792]{1,0:T(8,128)(2,1)S(1)}, u32[]{:S(2)}, u32[]{:S(2)}) collective-permute-start(bf16[448,1792]{1,0:T(8,128)(2,1)} %collective-permute-done.24), channel_id=1, source_target_pairs={{0,4},{4,0},{8,12},{12,8},{16,20},{20,16},{24,28},{28,24},{1,5},{5... | collective-permute-start | bytes 4816904 | tf_op jit(solution)/shard_map/ppermute | solution.py:37
  380.5 189.7 %collective-permute-start.16 = (bf16[448,1792]{1,0:T(8,128)(2,1)}, bf16[448,1792]{1,0:T(8,128)(2,1)}, u32[]{:S(2)}, u32[]{:S(2)}) collective-permute-start(bf16[448,1792]{1,0:T(8,128)(2,1)} %param.39), channel_id=1, source_target_pairs={{0,16},{4,20},{8,24},{12,28},{16,0},{20,4},{24,8},{28,12},{1,17},{... | collective-permute-start | bytes 4816904 | tf_op jit(solution)/shard_map/ppermute | solution.py:37
  411.8 162.8 %collective-permute-start.15 = (bf16[448,1792]{1,0:T(8,128)(2,1)}, bf16[448,1792]{1,0:T(8,128)(2,1)}, u32[]{:S(2)}, u32[]{:S(2)}) collective-permute-start(bf16[448,1792]{1,0:T(8,128)(2,1)} %param.39), channel_id=1, source_target_pairs={{0,8},{4,12},{8,0},{12,4},{16,24},{20,28},{24,16},{28,20},{1,9},{5... | collective-permute-start | bytes 4816904 | tf_op jit(solution)/shard_map/ppermute | solution.py:37
  414.5 171.0 %collective-permute-start.10 = (bf16[448,1792]{1,0:T(8,128)(2,1)}, bf16[448,1792]{1,0:T(8,128)(2,1)S(1)}, u32[]{:S(2)}, u32[]{:S(2)}) collective-permute-start(bf16[448,1792]{1,0:T(8,128)(2,1)} %param.38), channel_id=1, source_target_pairs={{0,24},{4,28},{8,16},{12,20},{16,8},{20,12},{24,0},{28,4},{1,25},{... | collective-permute-start | bytes 4816904 | tf_op jit(solution)/shard_map/ppermute | solution.py:37
  419.0 218.7 %collective-permute-start.9 = (bf16[448,1792]{1,0:T(8,128)(2,1)}, bf16[448,1792]{1,0:T(8,128)(2,1)}, u32[]{:S(2)}, u32[]{:S(2)}) collective-permute-start(bf16[448,1792]{1,0:T(8,128)(2,1)} %param.38), channel_id=1, source_target_pairs={{0,16},{4,20},{8,24},{12,28},{16,0},{20,4},{24,8},{28,12},{1,17},{... | collective-permute-start | bytes 4816904 | tf_op jit(solution)/shard_map/ppermute | solution.py:37
  468.4 112.2 %collective-permute-start.21 = (bf16[448,1792]{1,0:T(8,128)(2,1)}, bf16[448,1792]{1,0:T(8,128)(2,1)}, u32[]{:S(2)}, u32[]{:S(2)}) collective-permute-start(bf16[448,1792]{1,0:T(8,128)(2,1)} %collective-permute-done.17), channel_id=1, source_target_pairs={{0,4},{4,0},{8,12},{12,8},{16,20},{20,16},{24,28},{28,24},{1,5},{5... | collective-permute-start | bytes 4816904 | tf_op jit(solution)/shard_map/ppermute | solution.py:37
  570.2 73.4 %collective-permute-start.8 = (bf16[448,1792]{1,0:T(8,128)(2,1)}, bf16[448,1792]{1,0:T(8,128)(2,1)S(1)}, u32[]{:S(2)}, u32[]{:S(2)}) collective-permute-start(bf16[448,1792]{1,0:T(8,128)(2,1)} %param.38), channel_id=1, source_target_pairs={{0,8},{4,12},{8,0},{12,4},{16,24},{20,28},{24,16},{28,20},{1,9},{5... | collective-permute-start | bytes 4816904 | tf_op jit(solution)/shard_map/ppermute | solution.py:37
  574.6 72.5 %collective-permute-start.20 = (bf16[448,1792]{1,0:T(8,128)(2,1)}, bf16[448,1792]{1,0:T(8,128)(2,1)S(1)}, u32[]{:S(2)}, u32[]{:S(2)}) collective-permute-start(bf16[448,1792]{1,0:T(8,128)(2,1)} %collective-permute-done.16), channel_id=1, source_target_pairs={{0,4},{4,0},{8,12},{12,8},{16,20},{20,16},{24,28},{28,24},{1,5},{5... | collective-permute-start | bytes 4816904 | tf_op jit(solution)/shard_map/ppermute | solution.py:37
  580.6 70.9 %collective-permute-start.19 = (bf16[448,1792]{1,0:T(8,128)(2,1)}, bf16[448,1792]{1,0:T(8,128)(2,1)S(1)}, u32[]{:S(2)}, u32[]{:S(2)}) collective-permute-start(bf16[448,1792]{1,0:T(8,128)(2,1)} %collective-permute-done.15), channel_id=1, source_target_pairs={{0,4},{4,0},{8,12},{12,8},{16,20},{20,16},{24,28},{28,24},{1,5},{5... | collective-permute-start | bytes 4816904 | tf_op jit(solution)/shard_map/ppermute | solution.py:37
  585.5 96.1 %collective-permute-start.18 = (bf16[448,1792]{1,0:T(8,128)(2,1)}, bf16[448,1792]{1,0:T(8,128)(2,1)S(1)}, u32[]{:S(2)}, u32[]{:S(2)}) collective-permute-start(bf16[448,1792]{1,0:T(8,128)(2,1)} %param.39), channel_id=1, source_target_pairs={{0,4},{4,0},{8,12},{12,8},{16,20},{20,16},{24,28},{28,24},{1,5},{5... | collective-permute-start | bytes 4816904 | tf_op jit(solution)/shard_map/ppermute | solution.py:37
  637.7 78.4 %collective-permute-start.14 = (bf16[448,1792]{1,0:T(8,128)(2,1)S(1)}, bf16[448,1792]{1,0:T(8,128)(2,1)S(1)}, u32[]{:S(2)}, u32[]{:S(2)}) collective-permute-start(bf16[448,1792]{1,0:T(8,128)(2,1)S(1)} %collective-permute-done.10), channel_id=1, source_target_pairs={{0,4},{4,0},{8,12},{12,8},{16,20},{20,16},{24,28},{28,24},{1,5},{5... | collective-permute-start | bytes 4816904 | tf_op jit(solution)/shard_map/ppermute | solution.py:37
  643.6 106.9 %collective-permute-start.13 = (bf16[448,1792]{1,0:T(8,128)(2,1)}, bf16[448,1792]{1,0:T(8,128)(2,1)S(1)}, u32[]{:S(2)}, u32[]{:S(2)}) collective-permute-start(bf16[448,1792]{1,0:T(8,128)(2,1)} %collective-permute-done.9), channel_id=1, source_target_pairs={{0,4},{4,0},{8,12},{12,8},{16,20},{20,16},{24,28},{28,24},{1,5},{5... | collective-permute-start | bytes 4816904 | tf_op jit(solution)/shard_map/ppermute | solution.py:37
  647.1 137.8 %collective-permute-start.12 = (bf16[448,1792]{1,0:T(8,128)(2,1)S(1)}, bf16[448,1792]{1,0:T(8,128)(2,1)S(1)}, u32[]{:S(2)}, u32[]{:S(2)}) collective-permute-start(bf16[448,1792]{1,0:T(8,128)(2,1)S(1)} %collective-permute-done.8), channel_id=1, source_target_pairs={{0,4},{4,0},{8,12},{12,8},{16,20},{20,16},{24,28},{28,24},{1,5},{5... | collective-permute-start | bytes 4816904 | tf_op jit(solution)/shard_map/ppermute | solution.py:37
  651.5 164.0 %collective-permute-start.11 = (bf16[448,1792]{1,0:T(8,128)(2,1)}, bf16[448,1792]{1,0:T(8,128)(2,1)S(1)}, u32[]{:S(2)}, u32[]{:S(2)}) collective-permute-start(bf16[448,1792]{1,0:T(8,128)(2,1)} %param.38), channel_id=1, source_target_pairs={{0,4},{4,0},{8,12},{12,8},{16,20},{20,16},{24,28},{28,24},{1,5},{5... | collective-permute-start | bytes 4816904 | tf_op jit(solution)/shard_map/ppermute | solution.py:37
  (27 other events, 885.0 us)
Sparse Core Ops, SparseCore 0:
  150.7 66.3 reduce-scatter.4
  219.9 31.5 all-gather.1
  851.5 40.5 reduce-scatter.6
